TPU v7x, 128 devices: a whole 4x4x4 slice. The times are simulated.
128 devices in a mesh: example: 16 (over x, z_hi, core), proj: 8 (over z_lo, y).
Axes of the slice: x: 4, y: 4, z: 4 (z_hi: 2, z_lo: 2; z = z_hi * 2 + z_lo), core: 2. Of those that a mesh axis runs over, the one named last changes fastest.
Arguments:
- queries: bfloat16 [512, 131072], P('example', 'proj'), may hold values from -6 to 6
- store: bfloat16 [12288, 131072], P('example', 'proj'), may hold values from -6 to 6
- block_scale: float32 [12288, 1024], P('example', 'proj'), may hold values from 0.1 to 10
- query_inv: float32 [512], replicated, may hold values from 0.01 to 0.1
- train_inv: float32 [12288], P('example'), may hold values from 0.01 to 0.1
Outputs:
- scores: float32 [512, 12288], P('proj', 'example')
All inputs are finite; a program needn't handle non-finite values.
Results may differ from a plain program's by a relative error of at most 0.0029.
Values may be sent and summed in bfloat16 or wider, within the bound.
A program may use at most 192 MiB of HBM per device.

v0:
```python
import jax
import jax.numpy as jnp
from jax import lax
from jax.sharding import PartitionSpec as P


def body(queries, store, block_scale, query_inv, train_inv):
    row_count = store.shape[0]
    shard_width = store.shape[1]
    dequant = (
        (
            store.astype(jnp.float32).reshape(row_count, shard_width // 128, 128)
            * block_scale[:, :, None]
        )
        .reshape(row_count, shard_width)
        .astype(jnp.bfloat16)
    )
    partial_value = lax.dot_general(
        lax.all_gather(queries, "example", axis=0, tiled=True),
        dequant,
        (((1,), (1,)), ((), ())),
        preferred_element_type=jnp.float32,
    )
    summed = lax.psum_scatter(partial_value, "proj", scatter_dimension=0, tiled=True)
    query_rows = summed.shape[0]
    local_inv = lax.dynamic_slice_in_dim(
        query_inv, lax.axis_index("proj") * query_rows, query_rows, 0
    )
    return summed * local_inv[:, None] * train_inv[None, :]


def solution(mesh):
    placed = (P("example", "proj"), P("example", "proj"), P("example", "proj"), P(), P("example"))
    return jax.shard_map(
        body, mesh=mesh, in_specs=placed, out_specs=P("proj", "example"), check_vma=False
    )
```

profile of v0, /device:TPU:1, one launch (start us, length us, event | category | flops | bytes accessed | tf_op | source)
XLA Modules:
  0.0 232.1 jit_solution(1684152006405252906)
XLA Ops:
  6.5 0.0 all-gather.2.cloned.1.call-start
  6.5 0.7 all-gather.2.cloned.1.call-update
  7.3 0.0 reduce-scatter.4.cloned.1.call-start
  7.3 116.4 %all-gather.2.cloned.1.call-done = bf16[512,16384]{1,0:T(8,128)(2,1)} async-done(((bf16[32,16384]{1,0:T(8,128)(2,1)}), bf16[512,16384]{1,0:T(8,128)(2,1)}) %all-gather.2.cloned.1.call-update) | async-done | bytes 16777232 | tf_op jit(solution)/shard_map/all_gather | solution.py:19
  123.7 17.5 %mul.30 = f32[768,128,128]{2,1,0:T(8,128)} broadcast(f32[768,128]{1,0:T(8,128)} %param.7), dimensions={0,1} | broadcast | bytes 50724864 | tf_op jit(solution)/shard_map/mul | solution.py:12
  141.2 0.0 copy-start
  141.2 47.4 %fusion.3 = f32[512,768]{0,1:T(8,128)S(1)} fusion(bf16[512,16384]{1,0:T(8,128)(2,1)} %all-gather.2.cloned.1.call-done, f32[96,8,128,128]{3,2,1,0:T(8,128)} %bitcast.12, bf16[768,16384]{1,0:T(8,128)(2,1)} %param.6), kind=kOutput, calls=%fused_computation.3 | convolution fusion | flops 12922650624 | bytes 93847552 | tf_op jit(solution)/shard_map/dot_general | solution.py:18
  188.6 1.6 copy.9
  190.2 0.0 reduce-scatter.4.cloned.1.call-update
  190.3 0.8 dynamic_slice.3
  191.0 32.5 %reduce-scatter.4.cloned.1.call-done = f32[64,768]{1,0:T(8,128)} async-done(((f32[512,768]{1,0:T(8,128)}), f32[64,768]{1,0:T(8,128)}) %reduce-scatter.4.cloned.1.call-update) | async-done | bytes 196624 | tf_op jit(solution)/shard_map/reduce_scatter | solution.py:24
  223.5 0.0 copy-done
  223.5 1.7 multiply_multiply_fusion
Async XLA Ops:
  6.5 117.2 %all-gather.2.cloned.1.call-start = ((), (), s32[]{:S(2)}) async-start(), calls=%async_computation.1 | async-start | bytes 17825792 | tf_op jit(solution)/shard_map/all_gather | solution.py:19
  7.3 216.3 %reduce-scatter.4.cloned.1.call-start = ((), (), s32[]{:S(2)}) async-start(), calls=%async_computation.2 | async-start | bytes 1769472 | tf_op jit(solution)/shard_map/reduce_scatter | solution.py:24
  141.2 82.4 %copy-start = (f32[768]{0:T(1024)S(1)}, f32[768]{0:T(1024)}, u32[]{:S(2)}) copy-start(f32[768]{0:T(1024)} %param.9) | copy-start | bytes 9220
Sparse Core Ops, SparseCore 0:
  9.8 113.8 all-gather.1
  190.4 33.1 reduce-scatter.3
where the time goes:
time: 236 us; the launch traced here: 232 us
  waiting for transfers between devices  150 us (64%)
  matrix products  47.4 us (20%)
  local copies, waits for them, and re-layouts  19.9 us (8%)
  between operations  13.4 us (6%)
    all_gather x1, waiting for transfers between devices, body(): lax.all_gather(queries, 'example', axis=0, tiled=True)  116 us
    dot_general x1, matrix products, body(): lax.dot_general(lax.all_gather(queries, 'example', axis=0, tiled=True), d...  47.4 us
    reduce_scatter x1, waiting for transfers between devices, body(): lax.psum_scatter(partial_value, 'proj', scatter_dimension=0, tiled=True)  32.5 us
    mul x1, local copies, waits for them, and re-layouts, body(): store.astype(jnp.float32).reshape(row_count, shard_width // 128, 128)  17.5 us
  transfers between devices with their start and end apart: 2, of which 2 were waited for; matrix products, arithmetic and copies ran while one was open for 0% of the time, Pallas kernels for 0%

commit v1 on v0

v1 whole, which is shorter than its diff:
```python
import functools

import jax
import jax.numpy as jnp
from jax import lax
from jax.experimental import pallas as pl
from jax.experimental.pallas import tpu as pltpu
from jax.sharding import PartitionSpec as P

BF = jnp.bfloat16
F32 = jnp.float32
MESH = pl.DeviceIdType.MESH
NT = (((1,), (1,)), ((), ()))
STRIP = 16
PIECES = 16
WIDE = 8
AHEAD = 3
LAG = 3
B, F, Z, X2, ZB, ZF, ZX2 = range(7)


def kernel(
    q_hbm, s_hbm, scale_hbm, qinv_ref, tinv_ref, o_ref,
    qbuf, g, st, sc, acc, got,
    in_sem, st_sem, ici_sem, sib_sem, own_sem, out_sem, own_out, rs_sem, rs_out,
):
    rows, width = g.shape
    piece_w = width // WIDE
    half = width // 2
    e = lax.axis_index("example")
    p = lax.axis_index("proj")
    c = lax.rem(e, 2)
    zh = lax.rem(e // 2, 2)
    x = e // 4
    y = lax.rem(p, 4)
    zl = p // 4
    fdir = 1 - 2 * c
    xf = lax.rem(x + fdir + 4, 4)
    xb = lax.rem(x - fdir + 4, 4)
    x2 = lax.rem(x + 2, 4)
    zo = 1 - zh

    def at(x_, zh_, c_):
        return {"example": x_ * 4 + zh_ * 2 + c_, "proj": p}

    sib = at(x, zh, 1 - c)
    front = at(xf, zh, c)
    back = at(xb, zh, c)
    across = at(x, zo, c)
    owners = []
    for dz in range(2):
        for dy in range(4):
            if dz or dy:
                y_, zl_ = lax.rem(y + dy, 4), lax.rem(zl + dz, 2)
                owners.append((dz * 4 + dy - 1, zl_ * 4 + y_))

    def strip_row(h, x_, zh_, c_):
        chip = x_ * 2 + zh_
        return chip * 32 + c_ * 16 if h == 0 else 256 + c_ * 128 + chip * 16

    own_refs = [
        qbuf.at[pl.ds(pl.multiple_of(strip_row(h, x, zh, c), STRIP), STRIP), :]
        for h in range(2)
    ]
    own_in = [
        pltpu.make_async_copy(q_hbm.at[pl.ds(h * STRIP, STRIP), :], own_refs[h], in_sem.at[h])
        for h in range(2)
    ]
    scale_in = pltpu.make_async_copy(scale_hbm, sc, in_sem.at[2])

    def chunk_in(j):
        slot = lax.rem(j, 2)
        cols = pl.ds(pl.multiple_of(j * piece_w, piece_w), piece_w)
        return pltpu.make_async_copy(s_hbm.at[:, cols], st.at[slot], st_sem.at[slot])

    own_in[0].start()
    own_in[1].start()
    scale_in.start()
    chunk_in(0).start()
    chunk_in(1).start()

    barrier = pltpu.get_barrier_semaphore()
    for target in (sib, front, back, across):
        pl.semaphore_signal(barrier, inc=1, device_id=target, device_id_type=MESH)
    for _, owner in owners:
        pl.semaphore_signal(
            barrier, inc=1, device_id={"example": e, "proj": owner}, device_id_type=MESH
        )
    pl.semaphore_wait(barrier, 4 + len(owners))

    def place(n, x_, zh_):
        chip = x_ * 2 + zh_
        first = n < WIDE
        row = jnp.where(first, chip * 32 + c * 16, 256 + (n // 4 - 2) * 128 + chip * 16)
        col = jnp.where(first, n * piece_w, c * half + lax.rem(n, 4) * piece_w)
        return qbuf.at[
            pl.ds(pl.multiple_of(row, STRIP), STRIP),
            pl.ds(pl.multiple_of(col, piece_w), piece_w),
        ]

    def send(n, x_, zh_, target, recv):
        ref = place(n, x_, zh_)
        pltpu.make_async_remote_copy(
            ref, ref, out_sem.at[n], recv, device_id=target, device_id_type=MESH
        ).start()

    def arrived(n, x_, zh_, slot):
        ref = place(n, x_, zh_)
        pltpu.make_async_copy(ref, ref, ici_sem.at[n, slot]).wait()

    def spread_along_z(n):
        return lax.rem(n, 3) == 1

    def send_own(n):
        send(n, x, zh, front, ici_sem.at[n, B])
        send(n, x, zh, back, ici_sem.at[n, F])
        send(n, x, zh, across, ici_sem.at[n, Z])

    def stage1(n):
        along_z = spread_along_z(n)
        arrived(n, xb, zh, B)
        send(n, xb, zh, front, ici_sem.at[n, X2])

        @pl.when(along_z)
        def _():
            send(n, xb, zh, across, ici_sem.at[n, ZB])

        send(n, xb, zh, sib, sib_sem.at[n])
        arrived(n, x, zo, Z)

        @pl.when(jnp.logical_not(along_z))
        def _():
            send(n, x, zo, front, ici_sem.at[n, ZB])
            send(n, x, zo, back, ici_sem.at[n, ZF])

        send(n, x, zo, sib, sib_sem.at[n])
        arrived(n, xf, zh, F)

        @pl.when(along_z)
        def _():
            send(n, xf, zh, across, ici_sem.at[n, ZF])

        send(n, xf, zh, sib, sib_sem.at[n])

    def stage2(n):
        along_z = spread_along_z(n)
        arrived(n, xb, zo, ZB)

        @pl.when(jnp.logical_not(along_z))
        def _():
            send(n, xb, zo, front, ici_sem.at[n, ZX2])

        send(n, xb, zo, sib, sib_sem.at[n])
        arrived(n, x2, zh, X2)

        @pl.when(along_z)
        def _():
            send(n, x2, zh, across, ici_sem.at[n, ZX2])

        send(n, x2, zh, sib, sib_sem.at[n])
        arrived(n, xf, zo, ZF)
        send(n, xf, zo, sib, sib_sem.at[n])

    def stage3(n):
        arrived(n, x2, zo, ZX2)
        send(n, x2, zo, sib, sib_sem.at[n])

    def dequant(j):
        slot = lax.rem(j, 2)
        chunk_in(j).wait()
        blocks = piece_w // 128
        s = pltpu.roll(sc[...], lax.rem(128 - j * blocks, 128), 1)
        for r in range(0, rows, 128):
            for b in range(blocks):
                cols = pl.ds(pl.multiple_of(j * piece_w + b * 128, 128), 128)
                part = st[slot, r : r + 128, b * 128 : (b + 1) * 128].astype(F32)
                g[r : r + 128, cols] = (part * s[r : r + 128, b : b + 1]).astype(BF)

        @pl.when(j + 2 < WIDE)
        def _():
            chunk_in(j + 2).start()

    def multiply(n):
        pieces = qbuf.at[0 : 7 * STRIP, 0:piece_w]
        pltpu.make_async_copy(pieces, pieces, sib_sem.at[n]).wait()

        @pl.when(n < WIDE)
        def _():
            cols = pl.ds(pl.multiple_of(n * piece_w, piece_w), piece_w)
            acc[0:256, :] += lax.dot_general(
                qbuf[0:256, cols], g[:, cols], NT, preferred_element_type=F32
            )

        @pl.when(n >= WIDE)
        def _():
            at_row = pl.ds(pl.multiple_of(256 + (n // 4 - 2) * 128, 128), 128)
            for k in range(2):
                col = k * half + lax.rem(n, 4) * piece_w
                cols = pl.ds(pl.multiple_of(col, piece_w), piece_w)
                acc[at_row, :] += lax.dot_general(
                    qbuf[at_row, cols], g[:, cols], NT, preferred_element_type=F32
                )

    first_row, count, landing = (0, 256, 384), (32, 16, 16), (0, 32, 48)

    def send_sums(k):
        for slot, owner in owners:
            start = pl.multiple_of(first_row[k] + owner * count[k], STRIP)
            pltpu.make_async_remote_copy(
                acc.at[pl.ds(start, count[k]), :],
                got.at[slot, pl.ds(landing[k], count[k]), :],
                rs_out.at[k],
                rs_sem.at[k, slot],
                device_id={"example": e, "proj": owner},
                device_id_type=MESH,
            ).start()

    lane = lax.broadcasted_iota(jnp.int32, (64, qinv_ref.shape[0]), 1)
    row = lax.broadcasted_iota(jnp.int32, (64, qinv_ref.shape[0]), 0)
    qrow = qinv_ref[...].reshape(1, -1)
    qcol = jnp.sum(jnp.where(lane == row + p * 64, qrow, 0.0), axis=1, keepdims=True)
    trow = tinv_ref[...].reshape(1, -1)

    def finish(k):
        start = pl.multiple_of(first_row[k] + p * count[k], STRIP)
        total = acc[pl.ds(start, count[k]), :]
        for slot in range(7):
            ref = got.at[slot, pl.ds(landing[k], count[k]), :]
            pltpu.make_async_copy(ref, ref, rs_sem.at[k, slot]).wait()
            total += got[slot, landing[k] : landing[k] + count[k], :]
        pieces = [(0, 0), (16, 32)] if k == 0 else [(0, 16 if k == 1 else 48)]
        for here, there in pieces:
            o_ref[there : there + 16, :] = (
                total[here : here + 16, :] * qcol[there : there + 16, :] * trow
            )

    own_in[0].wait()
    own_in[1].wait()
    for h in range(2):
        if h == 1:
            for n in range(AHEAD):
                send_own(n)
        pltpu.make_async_remote_copy(
            own_refs[h], own_refs[h], own_out.at[h], own_sem.at[h],
            device_id=sib, device_id_type=MESH,
        ).start()
    acc[...] = jnp.zeros_like(acc)
    scale_in.wait()
    dequant(0)
    for h in range(2):
        ref = qbuf.at[pl.ds(pl.multiple_of(strip_row(h, x, zh, 1 - c), STRIP), STRIP), :]
        pltpu.make_async_copy(ref, ref, own_sem.at[h]).wait()

    def step(s, carry):
        @pl.when(s + AHEAD < PIECES)
        def _():
            send_own(s + AHEAD)

        @pl.when(s < PIECES)
        def _():
            stage1(s)

        @pl.when(s + 1 < WIDE)
        def _():
            dequant(s + 1)

        @pl.when((s >= 1) & (s < PIECES + 1))
        def _():
            stage2(s - 1)

        @pl.when((s >= 2) & (s < PIECES + 2))
        def _():
            stage3(s - 2)

        @pl.when(s >= LAG)
        def _():
            multiply(s - LAG)

        @pl.when(s == WIDE - 1 + LAG)
        def _():
            send_sums(0)

        @pl.when(s == WIDE + 3 + LAG)
        def _():
            send_sums(1)

        return carry

    lax.fori_loop(0, PIECES + LAG, step, 0)
    send_sums(2)
    finish(0)
    finish(1)
    finish(2)
    for n in range(PIECES):
        pieces = qbuf.at[0 : 14 * STRIP, 0:piece_w]
        pltpu.make_async_copy(pieces, pieces, out_sem.at[n]).wait()
    for h in range(2):
        pltpu.make_async_copy(own_refs[h], own_refs[h], own_out.at[h]).wait()
    for k in range(3):
        ref = acc.at[0 : 7 * count[k], :]
        pltpu.make_async_copy(ref, ref, rs_out.at[k]).wait()


def body(queries, store, block_scale, query_inv, train_inv):
    rows, width = store.shape
    n_query = query_inv.shape[0]
    hbm = pl.BlockSpec(memory_space=pl.ANY)
    vmem = pl.BlockSpec(memory_space=pltpu.VMEM)
    dma = pltpu.SemaphoreType.DMA
    return pl.pallas_call(
        kernel,
        out_shape=jax.ShapeDtypeStruct((n_query // 8, rows), F32),
        in_specs=[hbm, hbm, hbm, vmem, vmem],
        out_specs=vmem,
        scratch_shapes=[
            pltpu.VMEM((n_query, width), BF),
            pltpu.VMEM((rows, width), BF),
            pltpu.VMEM((2, rows, width // WIDE), BF),
            pltpu.VMEM((rows, width // 128), F32),
            pltpu.VMEM((n_query, rows), F32),
            pltpu.VMEM((7, n_query // 8, rows), F32),
            dma((3,)),
            dma((2,)),
            dma((PIECES, 7)),
            dma((PIECES,)),
            dma((2,)),
            dma((PIECES,)),
            dma((2,)),
            dma((3, 7)),
            dma((3,)),
        ],
        compiler_params=pltpu.CompilerParams(
            collective_id=0, has_side_effects=True, vmem_limit_bytes=60 << 20
        ),
        cost_estimate=pl.CostEstimate(
            flops=2 * n_query * rows * width,
            bytes_accessed=2 * rows * width,
            transcendentals=0,
        ),
        name="gather_score",
    )(queries, store, block_scale, query_inv, train_inv)


def solution(mesh):
    placed = (P("example", "proj"), P("example", "proj"), P("example", "proj"), P(), P("example"))
    return jax.shard_map(
        body, mesh=mesh, in_specs=placed, out_specs=P("proj", "example"), check_vma=False
    )
```

time: 236 us -> 98.6 us (0.42); the launches traced: 232 us -> 97.4 us
  waiting for transfers between devices: 150 us -> 0 us
  Pallas kernels: 0 us -> 95.8 us
  matrix products: 47.4 us -> 0 us
  local copies, waits for them, and re-layouts: 19.9 us -> 1.62 us
  between operations: 13.4 us -> 0.01 us
    all_gather x1 -> x0, waiting for transfers between devices: 116 us -> none  [body(): lax.all_gather(queries, 'example', axis=0, tiled=True)]
    pallas_call x0 -> x1, Pallas kernels: none -> 95.8 us  [body(): pl.pallas_call(kernel, out_shape=jax.ShapeDtypeStruct((n_query // 8, rows...]
    dot_general x1 -> x0, matrix products: 47.4 us -> none  [body(): lax.dot_general(lax.all_gather(queries, 'example', axis=0, tiled=True), d...]
    reduce_scatter x1 -> x0, waiting for transfers between devices: 32.5 us -> none  [body(): lax.psum_scatter(partial_value, 'proj', scatter_dimension=0, tiled=True)]
    mul x1 -> x0, local copies, waits for them, and re-layouts: 17.5 us -> none  [body(): store.astype(jnp.float32).reshape(row_count, shard_width // 128, 128)]
  transfers between devices with their start and end apart: 2 -> 0, of which waited for: 2 -> 0; matrix products, arithmetic and copies ran while one was open for 0% -> 0% of each run, Pallas kernels for 0% -> 0%
where the time goes in v1:
time: 98.6 us; the launch traced here: 97.4 us
  Pallas kernels  95.8 us (97%)
  local copies, waits for them, and re-layouts  1.62 us (2%)
    pallas_call x1, Pallas kernels, body(): pl.pallas_call(kernel, out_shape=jax.ShapeDtypeStruct((n_query // 8, rows...  95.8 us

profile of v1, /device:TPU:1, one launch (start us, length us, event | category | flops | bytes accessed | tf_op | source)
XLA Modules:
  0.0 97.4 jit_solution(15728886736455285379)
XLA Ops:
  0.0 95.8 %gather_score.1 = f32[64,768]{1,0:T(8,128)} custom-call(bf16[32,16384]{1,0:T(8,128)(2,1)} %q_hbm.1, bf16[768,16384]{1,0:T(8,128)(2,1)} %s_hbm.1, f32[768,128]{1,0:T(8,128)} %scale_hbm.1, f32[512]{0:T(512)} %qinv_ref.1, f32[768]{0:T(1024)} %tinv_ref.1), custom_call_target="tpu_custom_call" | custom-call | flops 12884901888 | bytes 25165824 | tf_op jit(solution)/shard_map/gather_score/pallas_call | solution.py:310
  95.8 1.6 %copy.7 = f32[64,768]{1,0:T(8,128)} copy(f32[64,768]{1,0:T(8,128)} %gather_score.1) | data formatting | bytes 393216

commit v2 on v1

--- a/solution.py
+++ b/solution.py
@@ -12,21 +12,22 @@
 MESH = pl.DeviceIdType.MESH
 NT = (((1,), (1,)), ((), ()))
 STRIP = 16
-PIECES = 16
 WIDE = 8
-AHEAD = 3
-LAG = 3
+PIECES = 2 * WIDE
+AHEAD = 4
+LAG2 = 4
+LAG3 = 8
+LAG = 9
 B, F, Z, X2, ZB, ZF, ZX2 = range(7)
 
 
 def kernel(
     q_hbm, s_hbm, scale_hbm, qinv_ref, tinv_ref, o_ref,
-    qbuf, g, st, sc, acc, got,
+    qbuf, g, st, sc, acc, sums, got,
     in_sem, st_sem, ici_sem, sib_sem, own_sem, out_sem, own_out, rs_sem, rs_out,
 ):
     rows, width = g.shape
     piece_w = width // WIDE
-    half = width // 2
     e = lax.axis_index("example")
     p = lax.axis_index("proj")
     c = lax.rem(e, 2)
@@ -55,8 +56,7 @@
                 owners.append((dz * 4 + dy - 1, zl_ * 4 + y_))
 
     def strip_row(h, x_, zh_, c_):
-        chip = x_ * 2 + zh_
-        return chip * 32 + c_ * 16 if h == 0 else 256 + c_ * 128 + chip * 16
+        return h * 256 + (x_ * 2 + zh_) * 32 + c_ * STRIP
 
     own_refs = [
         qbuf.at[pl.ds(pl.multiple_of(strip_row(h, x, zh, c), STRIP), STRIP), :]
@@ -90,9 +90,8 @@
 
     def place(n, x_, zh_):
         chip = x_ * 2 + zh_
-        first = n < WIDE
-        row = jnp.where(first, chip * 32 + c * 16, 256 + (n // 4 - 2) * 128 + chip * 16)
-        col = jnp.where(first, n * piece_w, c * half + lax.rem(n, 4) * piece_w)
+        row = (n // WIDE) * 256 + chip * 32 + c * STRIP
+        col = lax.rem(n, WIDE) * piece_w
         return qbuf.at[
             pl.ds(pl.multiple_of(row, STRIP), STRIP),
             pl.ds(pl.multiple_of(col, piece_w), piece_w),
@@ -109,12 +108,12 @@
         pltpu.make_async_copy(ref, ref, ici_sem.at[n, slot]).wait()
 
     def spread_along_z(n):
-        return lax.rem(n, 3) == 1
+        return (lax.rem(n + 2 * c, 5) == 1) | (lax.rem(n + 2 * c, 5) == 3)
 
     def send_own(n):
+        send(n, x, zh, across, ici_sem.at[n, Z])
         send(n, x, zh, front, ici_sem.at[n, B])
         send(n, x, zh, back, ici_sem.at[n, F])
-        send(n, x, zh, across, ici_sem.at[n, Z])
 
     def stage1(n):
         along_z = spread_along_z(n)
@@ -184,30 +183,21 @@
         pieces = qbuf.at[0 : 7 * STRIP, 0:piece_w]
         pltpu.make_async_copy(pieces, pieces, sib_sem.at[n]).wait()
 
-        @pl.when(n < WIDE)
-        def _():
-            cols = pl.ds(pl.multiple_of(n * piece_w, piece_w), piece_w)
-            acc[0:256, :] += lax.dot_general(
-                qbuf[0:256, cols], g[:, cols], NT, preferred_element_type=F32
-            )
-
-        @pl.when(n >= WIDE)
-        def _():
-            at_row = pl.ds(pl.multiple_of(256 + (n // 4 - 2) * 128, 128), 128)
-            for k in range(2):
-                col = k * half + lax.rem(n, 4) * piece_w
-                cols = pl.ds(pl.multiple_of(col, piece_w), piece_w)
-                acc[at_row, :] += lax.dot_general(
-                    qbuf[at_row, cols], g[:, cols], NT, preferred_element_type=F32
-                )
-
-    first_row, count, landing = (0, 256, 384), (32, 16, 16), (0, 32, 48)
+        group = pl.ds(pl.multiple_of(n // WIDE * 256, 256), 256)
+        cols = pl.ds(pl.multiple_of(lax.rem(n, WIDE) * piece_w, piece_w), piece_w)
+        acc[group, :] += lax.dot_general(
+            qbuf[group, cols], g[:, cols], NT, preferred_element_type=F32
+        )
+
+    first_row, count, landing = (0, 256), (32, 32), (0, 32)
 
     def send_sums(k):
+        group = pl.ds(first_row[k], 8 * count[k])
+        sums[group, :] = acc[group, :].astype(BF)
         for slot, owner in owners:
             start = pl.multiple_of(first_row[k] + owner * count[k], STRIP)
             pltpu.make_async_remote_copy(
-                acc.at[pl.ds(start, count[k]), :],
+                sums.at[pl.ds(start, count[k]), :],
                 got.at[slot, pl.ds(landing[k], count[k]), :],
                 rs_out.at[k],
                 rs_sem.at[k, slot],
@@ -227,9 +217,8 @@
         for slot in range(7):
             ref = got.at[slot, pl.ds(landing[k], count[k]), :]
             pltpu.make_async_copy(ref, ref, rs_sem.at[k, slot]).wait()
-            total += got[slot, landing[k] : landing[k] + count[k], :]
-        pieces = [(0, 0), (16, 32)] if k == 0 else [(0, 16 if k == 1 else 48)]
-        for here, there in pieces:
+            total += got[slot, landing[k] : landing[k] + count[k], :].astype(F32)
+        for here, there in ((0, 16 * k), (16, 32 + 16 * k)):
             o_ref[there : there + 16, :] = (
                 total[here : here + 16, :] * qcol[there : there + 16, :] * trow
             )
@@ -256,6 +245,14 @@
         def _():
             send_own(s + AHEAD)
 
+        @pl.when((s >= LAG3) & (s < PIECES + LAG3))
+        def _():
+            stage3(s - LAG3)
+
+        @pl.when((s >= LAG2) & (s < PIECES + LAG2))
+        def _():
+            stage2(s - LAG2)
+
         @pl.when(s < PIECES)
         def _():
             stage1(s)
@@ -264,14 +261,6 @@
         def _():
             dequant(s + 1)
 
-        @pl.when((s >= 1) & (s < PIECES + 1))
-        def _():
-            stage2(s - 1)
-
-        @pl.when((s >= 2) & (s < PIECES + 2))
-        def _():
-            stage3(s - 2)
-
         @pl.when(s >= LAG)
         def _():
             multiply(s - LAG)
@@ -280,24 +269,19 @@
         def _():
             send_sums(0)
 
-        @pl.when(s == WIDE + 3 + LAG)
-        def _():
-            send_sums(1)
-
         return carry
 
     lax.fori_loop(0, PIECES + LAG, step, 0)
-    send_sums(2)
+    send_sums(1)
     finish(0)
     finish(1)
-    finish(2)
     for n in range(PIECES):
         pieces = qbuf.at[0 : 14 * STRIP, 0:piece_w]
         pltpu.make_async_copy(pieces, pieces, out_sem.at[n]).wait()
     for h in range(2):
         pltpu.make_async_copy(own_refs[h], own_refs[h], own_out.at[h]).wait()
-    for k in range(3):
-        ref = acc.at[0 : 7 * count[k], :]
+    for k in range(2):
+        ref = sums.at[0 : 7 * count[k], :]
         pltpu.make_async_copy(ref, ref, rs_out.at[k]).wait()
 
 
@@ -318,7 +302,8 @@
             pltpu.VMEM((2, rows, width // WIDE), BF),
             pltpu.VMEM((rows, width // 128), F32),
             pltpu.VMEM((n_query, rows), F32),
-            pltpu.VMEM((7, n_query // 8, rows), F32),
+            pltpu.VMEM((n_query, rows), BF),
+            pltpu.VMEM((7, n_query // 8, rows), BF),
             dma((3,)),
             dma((2,)),
             dma((PIECES, 7)),
@@ -326,8 +311,8 @@
             dma((2,)),
             dma((PIECES,)),
             dma((2,)),
-            dma((3, 7)),
-            dma((3,)),
+            dma((2, 7)),
+            dma((2,)),
         ],
         compiler_params=pltpu.CompilerParams(
             collective_id=0, has_side_effects=True, vmem_limit_bytes=60 << 20

time: 98.6 us -> 82.7 us (0.84); the launches traced: 97.4 us -> 82.6 us
  Pallas kernels: 95.8 us -> 80.9 us
    pallas_call x1, Pallas kernels: 95.8 us -> 80.9 us  [body(): pl.pallas_call(kernel, out_shape=jax.ShapeDtypeStruct((n_query // 8, rows...]
where the time goes in v2:
time: 82.7 us; the launch traced here: 82.6 us
  Pallas kernels  80.9 us (98%)
  local copies, waits for them, and re-layouts  1.62 us (2%)
    pallas_call x1, Pallas kernels, body(): pl.pallas_call(kernel, out_shape=jax.ShapeDtypeStruct((n_query // 8, rows...  80.9 us

profile of v2, /device:TPU:1, one launch (start us, length us, event | category | flops | bytes accessed | tf_op | source)
XLA Modules:
  0.0 82.6 jit_solution(3579021164280160444)
XLA Ops:
  0.0 80.9 %gather_score.1 = f32[64,768]{1,0:T(8,128)} custom-call(bf16[32,16384]{1,0:T(8,128)(2,1)} %q_hbm.1, bf16[768,16384]{1,0:T(8,128)(2,1)} %s_hbm.1, f32[768,128]{1,0:T(8,128)} %scale_hbm.1, f32[512]{0:T(512)} %qinv_ref.1, f32[768]{0:T(1024)} %tinv_ref.1), custom_call_target="tpu_custom_call" | custom-call | flops 12884901888 | bytes 25165824 | tf_op jit(solution)/shard_map/gather_score/pallas_call | solution.py:294
  80.9 1.6 %copy.7 = f32[64,768]{1,0:T(8,128)} copy(f32[64,768]{1,0:T(8,128)} %gather_score.1) | data formatting | bytes 393216

commit v3 on v2

--- a/solution.py
+++ b/solution.py
@@ -14,10 +14,13 @@
 STRIP = 16
 WIDE = 8
 PIECES = 2 * WIDE
-AHEAD = 4
-LAG2 = 4
-LAG3 = 8
-LAG = 9
+AHEAD = 3
+LAG2 = 3
+LAG3 = 6
+LAG = 7
+TILE = 256
+MASK0 = 0b0010100101001010
+MASK1 = 0b0100101001010010
 B, F, Z, X2, ZB, ZF, ZX2 = range(7)
 
 
@@ -36,6 +39,7 @@
     y = lax.rem(p, 4)
     zl = p // 4
     fdir = 1 - 2 * c
+    mask = jnp.where(c == 0, MASK0, MASK1)
     xf = lax.rem(x + fdir + 4, 4)
     xb = lax.rem(x - fdir + 4, 4)
     x2 = lax.rem(x + 2, 4)
@@ -89,9 +93,9 @@
     pl.semaphore_wait(barrier, 4 + len(owners))
 
     def place(n, x_, zh_):
-        chip = x_ * 2 + zh_
-        row = (n // WIDE) * 256 + chip * 32 + c * STRIP
-        col = lax.rem(n, WIDE) * piece_w
+        late = jnp.where(n >= WIDE, 1, 0)
+        row = late * 256 + (x_ * 64 + zh_ * 32 + c * STRIP)
+        col = (n - late * WIDE) * piece_w
         return qbuf.at[
             pl.ds(pl.multiple_of(row, STRIP), STRIP),
             pl.ds(pl.multiple_of(col, piece_w), piece_w),
@@ -108,7 +112,7 @@
         pltpu.make_async_copy(ref, ref, ici_sem.at[n, slot]).wait()
 
     def spread_along_z(n):
-        return (lax.rem(n + 2 * c, 5) == 1) | (lax.rem(n + 2 * c, 5) == 3)
+        return (lax.shift_right_logical(mask, n) & 1) == 1
 
     def send_own(n):
         send(n, x, zh, across, ici_sem.at[n, Z])
@@ -179,31 +183,37 @@
         def _():
             chunk_in(j + 2).start()
 
-    def multiply(n):
+    def sibling_done(n):
         pieces = qbuf.at[0 : 7 * STRIP, 0:piece_w]
         pltpu.make_async_copy(pieces, pieces, sib_sem.at[n]).wait()
 
-        group = pl.ds(pl.multiple_of(n // WIDE * 256, 256), 256)
-        cols = pl.ds(pl.multiple_of(lax.rem(n, WIDE) * piece_w, piece_w), piece_w)
+    def multiply(n):
+        sibling_done(n)
+        late = jnp.where(n >= WIDE, 1, 0)
+        group = pl.ds(pl.multiple_of(late * 256, 256), 256)
+        cols = pl.ds(pl.multiple_of((n - late * WIDE) * piece_w, piece_w), piece_w)
         acc[group, :] += lax.dot_general(
             qbuf[group, cols], g[:, cols], NT, preferred_element_type=F32
         )
 
-    first_row, count, landing = (0, 256), (32, 32), (0, 32)
-
-    def send_sums(k):
-        group = pl.ds(first_row[k], 8 * count[k])
-        sums[group, :] = acc[group, :].astype(BF)
+    def send_sums(k, cols):
+        group = pl.ds(256 * k, 256)
+        sums[group, cols] = acc[group, cols].astype(BF)
+        part = k + cols.start // TILE
         for slot, owner in owners:
-            start = pl.multiple_of(first_row[k] + owner * count[k], STRIP)
+            start = pl.multiple_of(256 * k + owner * 32, 32)
             pltpu.make_async_remote_copy(
-                sums.at[pl.ds(start, count[k]), :],
-                got.at[slot, pl.ds(landing[k], count[k]), :],
-                rs_out.at[k],
-                rs_sem.at[k, slot],
+                sums.at[pl.ds(start, 32), cols],
+                got.at[slot, pl.ds(32 * k, 32), cols],
+                rs_out.at[part],
+                rs_sem.at[part, slot],
                 device_id={"example": e, "proj": owner},
                 device_id_type=MESH,
             ).start()
+
+    def sums_sent(k, cols):
+        ref = sums.at[0 : 7 * 32, cols]
+        pltpu.make_async_copy(ref, ref, rs_out.at[k + cols.start // TILE]).wait()
 
     lane = lax.broadcasted_iota(jnp.int32, (64, qinv_ref.shape[0]), 1)
     row = lax.broadcasted_iota(jnp.int32, (64, qinv_ref.shape[0]), 0)
@@ -211,16 +221,16 @@
     qcol = jnp.sum(jnp.where(lane == row + p * 64, qrow, 0.0), axis=1, keepdims=True)
     trow = tinv_ref[...].reshape(1, -1)
 
-    def finish(k):
-        start = pl.multiple_of(first_row[k] + p * count[k], STRIP)
-        total = acc[pl.ds(start, count[k]), :]
+    def finish(k, cols):
+        start = pl.multiple_of(256 * k + p * 32, 32)
+        total = acc[pl.ds(start, 32), cols]
         for slot in range(7):
-            ref = got.at[slot, pl.ds(landing[k], count[k]), :]
-            pltpu.make_async_copy(ref, ref, rs_sem.at[k, slot]).wait()
-            total += got[slot, landing[k] : landing[k] + count[k], :].astype(F32)
+            ref = got.at[slot, pl.ds(32 * k, 32), cols]
+            pltpu.make_async_copy(ref, ref, rs_sem.at[k + cols.start // TILE, slot]).wait()
+            total += got[slot, pl.ds(32 * k, 32), cols].astype(F32)
         for here, there in ((0, 16 * k), (16, 32 + 16 * k)):
-            o_ref[there : there + 16, :] = (
-                total[here : here + 16, :] * qcol[there : there + 16, :] * trow
+            o_ref[there : there + 16, cols] = (
+                total[here : here + 16, :] * qcol[there : there + 16, :] * trow[:, cols]
             )
 
     own_in[0].wait()
@@ -245,44 +255,52 @@
         def _():
             send_own(s + AHEAD)
 
+        @pl.when(s < PIECES)
+        def _():
+            stage1(s)
+
+        @pl.when(s + 1 < WIDE)
+        def _():
+            dequant(s + 1)
+
+        @pl.when((s >= LAG2) & (s < PIECES + LAG2))
+        def _():
+            stage2(s - LAG2)
+
         @pl.when((s >= LAG3) & (s < PIECES + LAG3))
         def _():
             stage3(s - LAG3)
 
-        @pl.when((s >= LAG2) & (s < PIECES + LAG2))
-        def _():
-            stage2(s - LAG2)
-
-        @pl.when(s < PIECES)
-        def _():
-            stage1(s)
-
-        @pl.when(s + 1 < WIDE)
-        def _():
-            dequant(s + 1)
-
         @pl.when(s >= LAG)
         def _():
             multiply(s - LAG)
 
         @pl.when(s == WIDE - 1 + LAG)
         def _():
-            send_sums(0)
+            send_sums(0, slice(0, rows))
 
         return carry
 
-    lax.fori_loop(0, PIECES + LAG, step, 0)
-    send_sums(1)
-    finish(0)
-    finish(1)
+    lax.fori_loop(0, PIECES + LAG - 1, step, 0)
+    sibling_done(PIECES - 1)
+    last = slice(width - piece_w, width)
+    tiles = [slice(t, t + TILE) for t in range(0, rows, TILE)]
+    for tile in tiles:
+        acc[256:512, tile] += lax.dot_general(
+            qbuf[256:512, last], g[tile, last], NT, preferred_element_type=F32
+        )
+        send_sums(1, tile)
+    finish(0, slice(0, rows))
+    for tile in tiles:
+        finish(1, tile)
     for n in range(PIECES):
         pieces = qbuf.at[0 : 14 * STRIP, 0:piece_w]
         pltpu.make_async_copy(pieces, pieces, out_sem.at[n]).wait()
     for h in range(2):
         pltpu.make_async_copy(own_refs[h], own_refs[h], own_out.at[h]).wait()
-    for k in range(2):
-        ref = sums.at[0 : 7 * count[k], :]
-        pltpu.make_async_copy(ref, ref, rs_out.at[k]).wait()
+    sums_sent(0, slice(0, rows))
+    for tile in tiles:
+        sums_sent(1, tile)
 
 
 def body(queries, store, block_scale, query_inv, train_inv):
@@ -311,8 +329,8 @@
             dma((2,)),
             dma((PIECES,)),
             dma((2,)),
-            dma((2, 7)),
-            dma((2,)),
+            dma((1 + rows // TILE, 7)),
+            dma((1 + rows // TILE,)),
         ],
         compiler_params=pltpu.CompilerParams(
             collective_id=0, has_side_effects=True, vmem_limit_bytes=60 << 20

time: 82.7 us -> 80.3 us (0.971)
  Pallas kernels: 80.9 us -> 78.5 us
    pallas_call x1, Pallas kernels: 80.9 us -> 78.5 us  [body(): pl.pallas_call(kernel, out_shape=jax.ShapeDtypeStruct((n_query // 8, rows...]
where the time goes in v3:
time: 80.3 us; the launch traced here: 80.2 us
  Pallas kernels  78.5 us (98%)
  local copies, waits for them, and re-layouts  1.62 us (2%)
    pallas_call x1, Pallas kernels, body(): pl.pallas_call(kernel, out_shape=jax.ShapeDtypeStruct((n_query // 8, rows...  78.5 us
    unnamed x1, local copies, waits for them, and re-layouts  1.62 us

profile of v3, /device:TPU:1, one launch (start us, length us, event | category | flops | bytes accessed | tf_op | source)
XLA Modules:
  0.0 80.2 jit_solution(12462851824974709897)
XLA Ops:
  0.0 78.5 %gather_score.1 = f32[64,768]{1,0:T(8,128)} custom-call(bf16[32,16384]{1,0:T(8,128)(2,1)} %q_hbm.1, bf16[768,16384]{1,0:T(8,128)(2,1)} %s_hbm.1, f32[768,128]{1,0:T(8,128)} %scale_hbm.1, f32[512]{0:T(512)} %qinv_ref.1, f32[768]{0:T(1024)} %tinv_ref.1), custom_call_target="tpu_custom_call" | custom-call | flops 12884901888 | bytes 25165824 | tf_op jit(solution)/shard_map/gather_score/pallas_call | solution.py:312
  78.6 1.6 %copy.7 = f32[64,768]{1,0:T(8,128)} copy(f32[64,768]{1,0:T(8,128)} %gather_score.1) | data formatting | bytes 393216

commit v4 on v3

--- a/solution.py
+++ b/solution.py
@@ -14,13 +14,13 @@
 STRIP = 16
 WIDE = 8
 PIECES = 2 * WIDE
-AHEAD = 3
+AHEAD = 4
 LAG2 = 3
 LAG3 = 6
 LAG = 7
 TILE = 256
-MASK0 = 0b0010100101001010
-MASK1 = 0b0100101001010010
+MASK0 = 0b0000101010101010
+MASK1 = 0b0000010101010101
 B, F, Z, X2, ZB, ZF, ZX2 = range(7)
 
 

time: 80.3 us -> 79.4 us (0.989)
  Pallas kernels: 78.5 us -> 77.6 us
    pallas_call x1, Pallas kernels: 78.5 us -> 77.6 us  [body(): pl.pallas_call(kernel, out_shape=jax.ShapeDtypeStruct((n_query // 8, rows...]
where the time goes in v4:
time: 79.4 us; the launch traced here: 79.2 us
  Pallas kernels  77.6 us (98%)
  local copies, waits for them, and re-layouts  1.62 us (2%)
    pallas_call x1, Pallas kernels, body(): pl.pallas_call(kernel, out_shape=jax.ShapeDtypeStruct((n_query // 8, rows...  77.6 us
    unnamed x1, local copies, waits for them, and re-layouts  1.62 us

profile of v4, /device:TPU:1, one launch (start us, length us, event | category | flops | bytes accessed | tf_op | source)
XLA Modules:
  0.0 79.2 jit_solution(15705728518936434426)
XLA Ops:
  0.0 77.6 %gather_score.1 = f32[64,768]{1,0:T(8,128)} custom-call(bf16[32,16384]{1,0:T(8,128)(2,1)} %q_hbm.1, bf16[768,16384]{1,0:T(8,128)(2,1)} %s_hbm.1, f32[768,128]{1,0:T(8,128)} %scale_hbm.1, f32[512]{0:T(512)} %qinv_ref.1, f32[768]{0:T(1024)} %tinv_ref.1), custom_call_target="tpu_custom_call" | custom-call | flops 12884901888 | bytes 25165824 | tf_op jit(solution)/shard_map/gather_score/pallas_call | solution.py:312
  77.6 1.6 %copy.7 = f32[64,768]{1,0:T(8,128)} copy(f32[64,768]{1,0:T(8,128)} %gather_score.1) | data formatting | bytes 393216

commit v5 on v4

--- a/solution.py
+++ b/solution.py
@@ -19,8 +19,8 @@
 LAG3 = 6
 LAG = 7
 TILE = 256
-MASK0 = 0b0000101010101010
-MASK1 = 0b0000010101010101
+MASK0 = 0b0000010101011010
+MASK1 = 0b0000001010110101
 B, F, Z, X2, ZB, ZF, ZX2 = range(7)
 
 

time: 79.4 us -> 80.6 us (1.015)
  Pallas kernels: 77.6 us -> 78.8 us
    pallas_call x1, Pallas kernels: 77.6 us -> 78.8 us  [body(): pl.pallas_call(kernel, out_shape=jax.ShapeDtypeStruct((n_query // 8, rows...]
where the time goes in v5:
time: 80.6 us; the launch traced here: 80.4 us
  Pallas kernels  78.8 us (98%)
  local copies, waits for them, and re-layouts  1.62 us (2%)
    pallas_call x1, Pallas kernels, body(): pl.pallas_call(kernel, out_shape=jax.ShapeDtypeStruct((n_query // 8, rows...  78.8 us
    unnamed x1, local copies, waits for them, and re-layouts  1.62 us

profile of v5, /device:TPU:1, one launch (start us, length us, event | category | flops | bytes accessed | tf_op | source)
XLA Modules:
  0.0 80.4 jit_solution(3238622654771759474)
XLA Ops:
  0.0 78.8 %gather_score.1 = f32[64,768]{1,0:T(8,128)} custom-call(bf16[32,16384]{1,0:T(8,128)(2,1)} %q_hbm.1, bf16[768,16384]{1,0:T(8,128)(2,1)} %s_hbm.1, f32[768,128]{1,0:T(8,128)} %scale_hbm.1, f32[512]{0:T(512)} %qinv_ref.1, f32[768]{0:T(1024)} %tinv_ref.1), custom_call_target="tpu_custom_call" | custom-call | flops 12884901888 | bytes 25165824 | tf_op jit(solution)/shard_map/gather_score/pallas_call | solution.py:312
  78.8 1.6 %copy.7 = f32[64,768]{1,0:T(8,128)} copy(f32[64,768]{1,0:T(8,128)} %gather_score.1) | data formatting | bytes 393216
